TPU v7x, 32 devices: a whole 2x2x4 slice. The times are simulated.
32 devices in a mesh: parts: 2 (over y), rep: 4 (over x, core), tp: 4 (over z).
Axes of the slice: x: 2, y: 2, z: 4, core: 2. Of those that a mesh axis runs over, the one named last changes fastest.
Arguments:
- queries: bfloat16 [192, 8192], P(('parts', 'rep'), 'tp'), parts along dimension 0, may hold values from -16 to 16, as said below
- new_kv: bfloat16 [192, 2048], P(('parts', 'rep'), 'tp'), parts along dimension 0, may hold values from -6 to 6
- kv_cache: bfloat16 [8, 96, 16, 2048], P(('parts', 'rep'), 'tp'), parts along dimension 0, may hold values from -16 to 16, as said below
- slot_owner: int32 [8, 96], P(('parts', 'rep'), 'tp'), parts along dimension 0, may hold values from -1 to 23
- slot_fill: int32 [8, 96], P(('parts', 'rep'), 'tp'), parts along dimension 0, may hold values from 1 to 16
- mig_source: int32 [8, 8], P(('parts', 'rep'), 'tp'), parts along dimension 0, may hold values from 0 to 3, as said below
- mig_slot: int32 [8, 8], P(('parts', 'rep'), 'tp'), parts along dimension 0, may hold values from 0 to 21
- adapter_id: int32 [192], P(('parts', 'rep')), parts along dimension 0, may hold values from 0 to 63
- out_weight: bfloat16 [8192, 8192], P('tp'), may hold values from -0.75 to 0.75
- shrink_weight: bfloat16 [64, 8192, 32], P(None, 'tp'), may hold values from -0.5 to 0.5
- expand_weight: bfloat16 [64, 32, 8192], P(None, None, 'tp'), may hold values from -0.5 to 0.5
Outputs:
- mixed: bfloat16 [192, 8192], P(('parts', 'rep'), 'tp'), parts along dimension 0
There are 2 independent parts, one for each index of `parts`. A program takes and returns all parts, laid end to end along the dimension named above; an argument that names none is the same for every part. Nothing has to cross between parts.
Inputs may be any that keep to these rules, and one draw needn't show every extreme that they name: queries stay within the range. `kv_cache`: cache entries stay within the range. `mig_source`: never the replica that receives the copy.
All inputs are finite; a program needn't handle non-finite values.
Results may differ from a plain program's by a relative error of at most 0.0053.
Values may be sent and summed in bfloat16 or wider, within the bound.
A program may use at most 128 MiB of HBM per device.

v0:
```python
import math

import jax
import jax.numpy as jnp
from jax import lax
from jax.sharding import PartitionSpec as P

H = 64
KVH = 8
HS = 128
BLK = 16
MIGS = 2


neg_big = -1e30
adapter_factor = 2.0


def joined(shard, axis, combine):
    everything = jax.tree.map(lambda part: lax.all_gather(part, axis), shard)
    leading = jax.tree.map(lambda part: part[0], everything)

    def turn(k, so_far):
        return combine(so_far, jax.tree.map(lambda part: part[k], everything))

    return lax.fori_loop(1, lax.axis_size(axis), turn, leading)


def local_partials(kv_pool, slot_rows, slot_len, whole_queries):
    slot_count = kv_pool.shape[0]
    row_count = whole_queries.shape[0]
    group_size = H // KVH
    score_scale = 1.0 / math.sqrt(HS)
    query_rows = whole_queries.reshape(row_count, KVH, group_size, HS)
    blocks = kv_pool.reshape(slot_count, BLK, KVH, 2, HS)
    key_portion = blocks[:, :, :, 0]
    value_part = blocks[:, :, :, 1]
    is_owned = slot_rows >= 0
    slot_query = query_rows[jnp.maximum(slot_rows, 0)]
    scores = (
        jnp.einsum("sgjd,stgd->sgjt", slot_query, key_portion, preferred_element_type=jnp.float32)
        * score_scale
    )
    is_valid = (jnp.arange(BLK)[None, :] < slot_len[:, None]) & is_owned[:, None]
    scores = jnp.where(is_valid[:, None, None, :], scores, neg_big)
    slot_max = jnp.max(scores, axis=3)
    weights = jnp.where(is_valid[:, None, None, :], jnp.exp(scores - slot_max[..., None]), 0.0)
    slot_sum = jnp.sum(weights, axis=3)
    slot_acc = jnp.einsum(
        "sgjt,stgd->sgjd",
        weights.astype(jnp.bfloat16),
        value_part,
        preferred_element_type=jnp.float32,
    )
    member = slot_rows[None, :] == jnp.arange(row_count)[:, None]
    local_max = jnp.max(jnp.where(member[:, :, None, None], slot_max[None], neg_big), axis=1)
    rescale_factor = jnp.where(
        is_owned[:, None, None], jnp.exp(slot_max - local_max[jnp.maximum(slot_rows, 0)]), 0.0
    )
    onehot = member.astype(jnp.float32)
    totals = jnp.einsum(
        "rs,sgj->rgj", onehot, rescale_factor * slot_sum, precision=lax.Precision.HIGHEST
    )
    weighted = jnp.einsum(
        "rs,sgjd->rgjd",
        onehot,
        rescale_factor[..., None] * slot_acc,
        precision=lax.Precision.HIGHEST,
    )
    return (
        local_max.reshape(row_count, H),
        totals.reshape(row_count, H),
        weighted.reshape(row_count, H, HS),
    )


def combine(earlier, later):
    best_score = jnp.maximum(earlier[0], later[0])
    first_ratio = jnp.exp(earlier[0] - best_score)
    second_ratio = jnp.exp(later[0] - best_score)
    totals = earlier[1] * first_ratio + later[1] * second_ratio
    weighted = earlier[2] * first_ratio[..., None] + later[2] * second_ratio[..., None]
    return (best_score, totals, weighted)


def body(
    queries,
    new_kv,
    kv_cache,
    slot_owner,
    slot_fill,
    mig_source,
    mig_slot,
    adapter_id,
    out_weight,
    shrink_weight,
    expand_weight,
):
    row_count = queries.shape[0]
    heads_here = queries.shape[1] // HS
    group_size = H // KVH
    score_scale = 1.0 / math.sqrt(HS)
    whole_queries, whole_new = (
        lax.all_gather(queries, "tp", axis=1, tiled=True),
        lax.all_gather(new_kv, "tp", axis=1, tiled=True),
    )
    local_pool = kv_cache[0]
    slot_count = local_pool.shape[0]
    wanted_source, wanted_slot = (
        lax.all_gather(mig_source, "rep", axis=0, tiled=True),
        lax.all_gather(mig_slot, "rep", axis=0, tiled=True),
    )
    current_replica = lax.axis_index("rep")
    is_mine = wanted_source == current_replica
    packed = jnp.where(
        is_mine[:, :, None, None], local_pool[wanted_slot], jnp.zeros((), local_pool.dtype)
    )
    arrived = lax.all_to_all(packed, "rep", split_axis=0, concat_axis=0, tiled=True)
    copied = arrived[mig_source[0], jnp.arange(mig_source.shape[1])]
    kv_pool = local_pool.at[slot_count - MIGS :].set(copied)
    local_max, totals, weighted = local_partials(
        kv_pool, slot_owner[0], slot_fill[0], whole_queries
    )
    first_head = lax.axis_index("tp") * heads_here
    best_all, total_all, weight_all = joined((local_max, totals, weighted), "tp", combine)
    best_score = lax.dynamic_slice_in_dim(best_all, first_head, heads_here, 1)
    totals = lax.dynamic_slice_in_dim(total_all, first_head, heads_here, 1)
    weighted = lax.dynamic_slice_in_dim(weight_all, first_head, heads_here, 1)
    local_query = queries.reshape(row_count, heads_here, HS)
    groups = (first_head + jnp.arange(heads_here)) // group_size
    fresh_kv = jnp.take(whole_new.reshape(row_count, KVH, 2, HS), groups, axis=1)
    new_score = (
        jnp.einsum(
            "rhd,rhd->rh", local_query, fresh_kv[:, :, 0], preferred_element_type=jnp.float32
        )
        * score_scale
    )
    top_score = jnp.maximum(best_score, new_score)
    old_weight = jnp.exp(best_score - top_score)
    new_weight = jnp.exp(new_score - top_score)
    numerator = weighted * old_weight[..., None] + new_weight[..., None] * fresh_kv[:, :, 1].astype(
        jnp.float32
    )
    denominator = totals * old_weight + new_weight
    attention = (
        (numerator / denominator[..., None])
        .reshape(row_count, heads_here * HS)
        .astype(jnp.bfloat16)
    )
    base_output = lax.psum_scatter(
        lax.dot_general(
            out_weight, attention, (((0,), (1,)), ((), ())), preferred_element_type=jnp.float32
        ),
        "tp",
        scatter_dimension=0,
        tiled=True,
    ).T
    adapters_all = shrink_weight.shape[0]
    shrink_all = jnp.einsum(
        "rk,akq->raq", attention, shrink_weight, preferred_element_type=jnp.float32
    )
    chosen = adapter_id[:, None] == jnp.arange(adapters_all, dtype=jnp.int32)[None, :]
    partial_value = jnp.sum(jnp.where(chosen[:, :, None], shrink_all, 0.0), axis=1)
    shrink = lax.psum(partial_value, "tp").astype(jnp.bfloat16)
    spread = jnp.where(chosen[:, :, None], shrink[:, None, :], jnp.zeros((), jnp.bfloat16)).reshape(
        row_count, -1
    )
    expand_matrix = jnp.dot(
        spread, expand_weight.reshape(spread.shape[1], -1), preferred_element_type=jnp.float32
    )
    return (base_output + adapter_factor * expand_matrix).astype(jnp.bfloat16)


def solution(mesh):
    return jax.shard_map(
        body,
        mesh=mesh,
        in_specs=(
            P(("parts", "rep"), "tp"),
            P(("parts", "rep"), "tp"),
            P(("parts", "rep"), "tp", None, None),
            P(("parts", "rep"), "tp"),
            P(("parts", "rep"), "tp"),
            P(("parts", "rep"), "tp"),
            P(("parts", "rep"), "tp"),
            P(("parts", "rep")),
            P("tp", None),
            P(None, "tp", None),
            P(None, None, "tp"),
        ),
        out_specs=P(("parts", "rep"), "tp"),
        check_vma=False,
    )
```

profile of v0, /device:TPU:0, one launch (start us, length us, event | category | flops | bytes accessed | tf_op | source)
XLA Modules:
  0.0 188.7 jit_solution(17908082220637885088)
XLA Ops:
  6.5 1.5 copy.167
  8.0 6.1 %all-gather.1 = s32[4,1,2]{2,1,0:T(1,128)S(1)} all-gather(s32[1,1,2]{2,1,0:T(1,128)S(1)} %bitcast.121), channel_id=1, replica_groups=mesh['parts'=2,'rep'=4,'tp'=4] {'rep'}, dimensions={0}, use_global_device_ids=true | all-gather | bytes 40 | tf_op jit(solution)/shard_map/all_gather | solution.py:111
  14.4 5.3 %all-gather = s32[4,1,2]{2,1,0:T(1,128)S(1)} all-gather(s32[1,1,2]{2,1,0:T(1,128)S(1)} %bitcast.122), channel_id=1, replica_groups=mesh['parts'=2,'rep'=4,'tp'=4] {'rep'}, dimensions={0}, use_global_device_ids=true | all-gather | bytes 40 | tf_op jit(solution)/shard_map/all_gather | solution.py:110
  20.3 0.9 broadcast_select_fusion
  21.2 3.5 %all-to-all-start = ((bf16[4,2,16,2048]{3,2,1,0:T(8,128)(2,1)}), bf16[4,2,16,2048]{3,2,1,0:T(8,128)(2,1)S(1)}, u32[]{:S(2)}, u32[]{:S(2)}) async-start(bf16[4,2,16,2048]{3,2,1,0:T(8,128)(2,1)} %broadcast_select_fusion), calls=%async_computation | async-start | bytes 1048576 | tf_op jit(solution)/shard_map/all_to_all | solution.py:118
  24.8 15.3 %all_gather.21 = bf16[24,8192]{1,0:T(8,128)(2,1)S(1)} all-gather(bf16[24,2048]{1,0:T(8,128)(2,1)S(1)} %copy-done.1), channel_id=1, replica_groups=mesh['parts'=2,'rep'=4,'tp'=4] {'tp'}, dimensions={1}, use_global_device_ids=true | all-gather | bytes 491520 | tf_op jit(solution)/shard_map/all_gather | solution.py:104
  41.5 1.1 reshape.256
  42.6 3.3 %fusion.64 = (bf16[24,16,8,1,128]{4,3,2,1,0:T(2,128)(2,1)}, bf16[24,16,8,1,128]{4,3,2,1,0:T(2,128)(2,1)S(1)}) fusion(bf16[24,16,8,2,128]{4,3,2,1,0:T(2,128)(2,1)S(1)} %reshape.256), kind=kLoop, calls=%fused_computation.102 | loop fusion | bytes 3145728 | tf_op jit(solution)/shard_map/slice | solution.py:37
  48.1 0.7 convolution_multiply_fusion
  48.9 0.9 fusion.28
  49.8 1.0 copy.100
  50.9 13.6 %all_gather.27 = bf16[24,2048]{1,0:T(8,128)(2,1)S(1)} all-gather(bf16[24,512]{1,0:T(8,128)(2,1)S(1)} %copy-done.3), channel_id=1, replica_groups=mesh['parts'=2,'rep'=4,'tp'=4] {'tp'}, dimensions={1}, use_global_device_ids=true | all-gather | bytes 122880 | tf_op jit(solution)/shard_map/all_gather | solution.py:105
  66.1 14.0 %all_gather.25 = f32[4,24,64]{2,1,0:T(8,128)S(1)} all-gather(f32[1,24,64]{2,1,0:T(8,128)S(1)} %convolution_bitcast_fusion.1), channel_id=1, replica_groups=mesh['parts'=2,'rep'=4,'tp'=4] {'tp'}, dimensions={0}, use_global_device_ids=true | all-gather | bytes 30720 | tf_op jit(solution)/shard_map/all_gather | solution.py:20
  80.0 13.7 %all_gather.24 = f32[4,24,64]{2,1,0:T(8,128)S(1)} all-gather(f32[1,24,64]{2,1,0:T(8,128)S(1)} %copy.95), channel_id=1, replica_groups=mesh['parts'=2,'rep'=4,'tp'=4] {'tp'}, dimensions={0}, use_global_device_ids=true | all-gather | bytes 30720 | tf_op jit(solution)/shard_map/all_gather | solution.py:20
  93.7 24.3 %all-gather.4.cloned.1.call-done = f32[4,24,64,128]{3,2,1,0:T(8,128)} async-done(((f32[1,24,64,128]{3,2,1,0:T(8,128)}), f32[4,24,64,128]{3,2,1,0:T(8,128)}) %all-gather.4.cloned.1.call-update) | async-done | bytes 3145744 | tf_op jit(solution)/shard_map/all_gather | solution.py:20
  118.1 1.2 slice_bitcast_fusion
  119.3 5.7 %while.20 = (s32[]{:T(128)}, f32[24,64]{1,0:T(8,128)S(1)}, f32[24,64]{1,0:T(8,128)S(1)}, f32[24,64,128]{2,1,0:T(8,128)S(1)}, f32[4,24,64]{2,1,0:T(8,128)S(1)}, /...) while((s32[]{:T(128)}, f32[24,64]{1,0:T(8,128)S(1)}, ...), condition=%wide.region_4.5_spmd, body=%wide.region_3.4_spmd.sunk | while | flops 599045 | bytes 2420887 | solution.py:26
  119.3 1.9 fusion.73
  121.2 1.9 fusion.73
  123.1 1.9 fusion.73
  125.9 13.7 %convolution_bitcast_fusion = f32[8192,24]{0,1:T(8,128)} fusion(bf16[2048,8192]{1,0:T(8,128)(2,1)} %param.23, bf16[24,16,128]{2,0,1:T(8,128)(2,1)S(1)} %fusion.38), kind=kOutput, calls=%fused_computation.13 | convolution fusion | flops 805306368 | bytes 34439168 | tf_op jit(solution)/shard_map/dot_general | solution.py:151
  139.8 12.3 %fusion.23 = f32[24,32]{0,1:T(8,128)S(1)} fusion(bf16[24,2048,1]{1,0,2:T(8,128)(2,1)S(1)} %reshape.314, bf16[64,2048,32]{1,2,0:T(8,128)(2,1)} %param.24, pred[24,64]{1,0:T(8,128)(4,1)S(1)} %iota_compare_fusion), kind=kOutput, calls=%fused_computation.26 | convolution fusion | flops 201424128 | bytes 8491520 | tf_op jit(solution)/shard_map/rk,akq->raq/dot_general | solution.py:159
  152.2 16.8 %psum.7 = bf16[24,32]{0,1:T(8,128)(2,1)S(1)} all-reduce(f32[24,32]{0,1:T(8,128)S(1)} %fusion.23), channel_id=1, replica_groups=mesh['parts'=2,'rep'=4,'tp'=4] {'tp'}, use_global_device_ids=true, to_apply=%region_7.8 | all-reduce | flops 768 | bytes 4608 | tf_op jit(solution)/shard_map/psum | solution.py:164
  169.0 12.9 %fusion.16 = bf16[24,2048]{1,0:T(8,128)(2,1)} fusion(bf16[64,32,2048]{2,1,0:T(8,128)(2,1)} %param.25, f32[2048,24]{0,1:T(8,128)} %reduce-scatter.2.cloned.1.call-done, pred[24,64]{1,0:T(8,128)(4,1)S(1)} %iota_compare_fusion, bf16[24,32]{0,1:T(8,128)(2,1)S(1)} %psum.7), kind=kOutput, calls=%fused_computation.21 | convolution fusion | flops 201523200 | bytes 8686592 | tf_op jit(solution)/shard_map/dot_general | solution.py:168
  (80 shorter events, 7.1 us)
Async XLA Ops:
  6.5 18.2 %copy-start.1 = (bf16[24,2048]{1,0:T(8,128)(2,1)S(1)}, bf16[24,2048]{1,0:T(8,128)(2,1)}, u32[]{:S(2)}) copy-start(bf16[24,2048]{1,0:T(8,128)(2,1)} %param.15) | copy-start | bytes 294916
  6.5 18.2 %copy-start.4 = (s32[1,24]{1,0:T(1,128)S(1)}, s32[1,24]{1,0:T(1,128)}, u32[]{:S(2)}) copy-start(s32[1,24]{1,0:T(1,128)} %param.18) | copy-start | bytes 292
  6.5 7.8 %copy-start.8 = (s32[1,2]{1,0:T(1,128)S(1)}, s32[1,2]{1,0:T(1,128)}, u32[]{:S(2)}) copy-start(s32[1,2]{1,0:T(1,128)} %param.20) | copy-start | bytes 28
  6.5 1.5 copy-start.7
  8.0 32.8 %copy-start.10 = (s32[1,24]{1,0:T(1,128)S(1)}, s32[1,24]{1,0:T(1,128)}, u32[]{:S(2)}) copy-start(s32[1,24]{1,0:T(1,128)} %param.19) | copy-start | bytes 292
  21.2 19.7 %all-to-all-start = ((bf16[4,2,16,2048]{3,2,1,0:T(8,128)(2,1)}), bf16[4,2,16,2048]{3,2,1,0:T(8,128)(2,1)S(1)}, u32[]{:S(2)}, u32[]{:S(2)}) async-start(bf16[4,2,16,2048]{3,2,1,0:T(8,128)(2,1)} %broadcast_select_fusion), calls=%async_computation | async-start | bytes 1048576 | tf_op jit(solution)/shard_map/all_to_all | solution.py:118
  24.7 93.4 %all-gather.4.cloned.1.call-start = ((), (), s32[]{:S(2)}) async-start(), calls=%async_computation.2 | async-start | bytes 3932160 | tf_op jit(solution)/shard_map/all_gather | solution.py:20
  40.8 0.7 copy-start.5
  45.9 2.1 %copy-start.6 = (pred[24]{0:T(512)(128)(4,1)S(1)}, pred[24]{0:T(512)(128)(4,1)}, u32[]{:S(2)}) copy-start(pred[24]{0:T(512)(128)(4,1)} %copy-done.5) | copy-start | bytes 76
  45.9 2.2 %copy-start = (bf16[24,16,8,1,128]{4,3,2,1,0:T(2,128)(2,1)S(1)}, bf16[24,16,8,1,128]{4,3,2,1,0:T(2,128)(2,1)}, u32[]{:S(2)}) copy-start(bf16[24,16,8,1,128]{4,3,2,1,0:T(2,128)(2,1)} %get-tuple-element.235) | copy-start | bytes 2359300
  48.1 2.8 %copy-start.3 = (bf16[24,512]{1,0:T(8,128)(2,1)S(1)}, bf16[24,512]{1,0:T(8,128)(2,1)}, u32[]{:S(2)}) copy-start(bf16[24,512]{1,0:T(8,128)(2,1)} %param.16) | copy-start | bytes 73732
  48.1 16.5 %copy-start.2 = (bf16[24,2048]{1,0:T(8,128)(2,1)S(1)}, bf16[24,2048]{1,0:T(8,128)(2,1)}, u32[]{:S(2)}) copy-start(bf16[24,2048]{1,0:T(8,128)(2,1)} %param.15) | copy-start | bytes 294916
  50.9 118.1 %reduce-scatter.2.cloned.1.call-start = ((), (), s32[]{:S(2)}) async-start(), calls=%async_computation.3 | async-start | bytes 983040 | tf_op jit(solution)/shard_map/reduce_scatter | solution.py:150
  125.9 13.8 %copy-start.9 = (s32[24]{0:T(128)S(1)}, s32[24]{0:T(128)}, u32[]{:S(2)}) copy-start(s32[24]{0:T(128)} %param.22) | copy-start | bytes 292
Sparse Core Ops, SparseCore 0:
  51.0 67.0 all-gather.3
  139.8 22.1 reduce-scatter.1
where the time goes:
time: 189 us
  blocking collectives  84.7 us (45%)
  matrix products  41.4 us (22%)
  waiting for transfers between devices  24.4 us (13%)
  between operations  13.8 us (7%)
  local copies, waits for them, and re-layouts  12.6 us (7%)
  other arithmetic  8.18 us (4%)
  starting transfers between devices  3.55 us (2%)
    all_gather x2, blocking collectives, joined(): everything = jax.tree.map(lambda part: lax.all_gather(part, axis), shard)  27.7 us
    all_gather x1, waiting for transfers between devices, joined(): everything = jax.tree.map(lambda part: lax.all_gather(part, axis), shard)  24.3 us
    psum x1, blocking collectives, body(): shrink = lax.psum(partial_value, 'tp').astype(jnp.bfloat16)  16.8 us
    all_gather x1, blocking collectives, body(): lax.all_gather(queries, 'tp', axis=1, tiled=True)  15.3 us
    dot_general x1, matrix products, body(): lax.dot_general(out_weight, attention, (((0,), (1,)), ((), ())), preferre...  13.7 us
    all_gather x1, blocking collectives, body(): lax.all_gather(new_kv, 'tp', axis=1, tiled=True)  13.6 us
    dot_general x1, matrix products, body(): jnp.dot(spread, expand_weight.reshape(spread.shape[1], -1), preferred_ele...  12.9 us
    dot_general x1, matrix products, body(): jnp.einsum('rk,akq->raq', attention, shrink_weight, preferred_element_typ...  12.3 us
  transfers between devices with their start and end apart: 3, of which 1 were waited for; matrix products, arithmetic and copies ran while one was open for 8% of the time, Pallas kernels for 0%

commit v1 on v0

--- a/solution.py
+++ b/solution.py
@@ -1,8 +1,11 @@
+import functools
 import math
 
 import jax
 import jax.numpy as jnp
 from jax import lax
+from jax.experimental import pallas as pl
+from jax.experimental.pallas import tpu as pltpu
 from jax.sharding import PartitionSpec as P
 
 H = 64
@@ -171,9 +174,419 @@
     return (base_output + adapter_factor * expand_matrix).astype(jnp.bfloat16)
 
 
+def remote(src, dst, send_sem, recv_sem, axis, target):
+    return pltpu.make_async_remote_copy(
+        src_ref=src,
+        dst_ref=dst,
+        send_sem=send_sem,
+        recv_sem=recv_sem,
+        device_id={axis: target},
+        device_id_type=pl.DeviceIdType.MESH,
+    )
+
+
+def layer_kernel(
+    n_tp,
+    n_rep,
+    rank,
+    q_ref,
+    new_ref,
+    kv_hbm,
+    column_row_ref,
+    mig_source_ref,
+    mig_slot_ref,
+    adapter_ref,
+    out_w_hbm,
+    shrink_w_hbm,
+    expand_w_hbm,
+    result_ref,
+    kv,
+    out_w,
+    shrink_w,
+    expand_w,
+    q_all,
+    slot_in,
+    slot_smem,
+    mig_out,
+    mig_in,
+    acc_out,
+    acc_in,
+    stat_out,
+    stat_in,
+    shrink_out,
+    shrink_in,
+    base_out,
+    base_in,
+    kv_sem,
+    weight_sem,
+    smem_sem,
+    q_send,
+    q_recv,
+    slot_send,
+    slot_recv,
+    mig_send,
+    mig_recv,
+    acc_send,
+    acc_recv,
+    stat_send,
+    stat_recv,
+    shrink_send,
+    shrink_recv,
+    base_send,
+    base_recv,
+):
+    f32, bf16 = jnp.float32, jnp.bfloat16
+    tp = lax.axis_index("tp")
+    rep = lax.axis_index("rep")
+    rows = result_ref.shape[0]
+    here = result_ref.shape[1]
+    half = here // 2
+    slots = kv.shape[0]
+    migs = mig_out.shape[1]
+    own_rows = q_ref.shape[0]
+    heads_here = own_rows // rows
+    group_size = H // KVH
+    groups_here = heads_here // group_size
+    group_rows = rows * group_size
+    score_scale = 1.0 / math.sqrt(HS)
+    tp_peers = [lax.rem(tp + d, n_tp) for d in range(1, n_tp)]
+    rep_peers = [lax.rem(rep + d, n_rep) for d in range(1, n_rep)]
+    kv_copy = pltpu.make_async_copy(kv_hbm, kv, kv_sem)
+    kv_copy.start()
+    barrier = pltpu.get_barrier_semaphore()
+    for peer in tp_peers:
+        pl.semaphore_signal(
+            barrier, inc=1, device_id={"tp": peer}, device_id_type=pl.DeviceIdType.MESH
+        )
+    for peer in rep_peers:
+        pl.semaphore_signal(
+            barrier, inc=1, device_id={"rep": peer}, device_id_type=pl.DeviceIdType.MESH
+        )
+
+    def block(k):
+        return pl.ds(pl.multiple_of(k * here, here), here)
+
+    def q_rows(k):
+        return pl.ds(pl.multiple_of(k * own_rows, 16), own_rows)
+
+    weight_copies = [pltpu.make_async_copy(shrink_w_hbm, shrink_w, weight_sem.at[0])]
+    order = tp_peers + [tp]
+    for i, peer in enumerate(order):
+        weight_copies.append(
+            pltpu.make_async_copy(
+                out_w_hbm.at[:, block(peer)], out_w.at[:, block(peer)], weight_sem.at[1 + i]
+            )
+        )
+    weight_copies.append(pltpu.make_async_copy(expand_w_hbm, expand_w, weight_sem.at[1 + n_tp]))
+    for copy in weight_copies:
+        copy.start()
+
+    q_all[q_rows(tp), :] = q_ref[...]
+    slot_in[pl.ds(rep, 1)] = mig_slot_ref[...]
+    mig_in[pl.ds(rep, 1)] = jnp.zeros((1,) + mig_in.shape[1:], bf16)
+    pl.semaphore_wait(barrier, n_tp - 1 + n_rep - 1)
+
+    slot_copies = [
+        remote(
+            mig_slot_ref, slot_in.at[pl.ds(rep, 1)], slot_send.at[d], slot_recv.at[d], "rep", peer
+        )
+        for d, peer in enumerate(rep_peers)
+    ]
+    for copy in slot_copies:
+        copy.start()
+    q_copies = [
+        remote(q_ref, q_all.at[q_rows(tp), :], q_send.at[d], q_recv.at[d], "tp", peer)
+        for d, peer in enumerate(tp_peers)
+    ]
+    for copy in q_copies[::-1]:
+        copy.start()
+
+    kv_copy.wait()
+    for copy in slot_copies:
+        copy.wait()
+    to_smem = pltpu.make_async_copy(slot_in, slot_smem, smem_sem)
+    to_smem.start()
+    to_smem.wait()
+    mig_copies = []
+    for d, peer in enumerate(rep_peers):
+        for k in range(migs):
+            mig_out[d, k] = kv[slot_smem[peer, 0, k]]
+        copy = remote(
+            mig_out.at[d], mig_in.at[rep], mig_send.at[d], mig_recv.at[d], "rep", peer
+        )
+        copy.start()
+        mig_copies.append(copy)
+
+    own_query = q_ref[...].astype(f32)
+    fresh = new_ref[...].astype(f32)
+    fresh_key = jnp.concatenate(
+        [
+            fresh[:, g * 2 * HS : (g * 2 + 1) * HS]
+            for g in range(groups_here)
+            for _ in range(group_size)
+        ],
+        axis=0,
+    )
+    fresh_value = jnp.concatenate(
+        [
+            fresh[:, (g * 2 + 1) * HS : (g * 2 + 2) * HS]
+            for g in range(groups_here)
+            for _ in range(group_size)
+        ],
+        axis=0,
+    )
+    new_score = jnp.sum(own_query * fresh_key, axis=1, keepdims=True) * score_scale
+    row_index = lax.rem(lax.broadcasted_iota(jnp.int32, (group_rows, slots * BLK), 0), rows)
+    member = row_index == column_row_ref[...]
+
+    for copy in q_copies:
+        copy.wait()
+    for copy in mig_copies:
+        copy.wait()
+    for k in range(migs):
+        kv[slots - migs + k] = mig_in[mig_source_ref[0, k], k]
+
+    acc_copies = []
+    lane = lax.broadcasted_iota(jnp.int32, (group_rows, HS), 1)
+    for d, peer in enumerate(order):
+        stats = []
+        for j in range(groups_here):
+            group = peer * groups_here + j
+            query = q_all[pl.ds(pl.multiple_of(group * group_rows, 16), group_rows), :]
+            key_at = pl.ds(pl.multiple_of(group * 2 * HS, HS), HS)
+            value_at = pl.ds(pl.multiple_of(group * 2 * HS + HS, HS), HS)
+            key = kv[:, :, key_at].reshape(slots * BLK, HS)
+            value = kv[:, :, value_at].reshape(slots * BLK, HS)
+            score = (
+                lax.dot_general(
+                    query, key, (((1,), (1,)), ((), ())), preferred_element_type=f32
+                )
+                * score_scale
+            )
+            score = jnp.where(member, score, neg_big)
+            top = jnp.max(score, axis=1, keepdims=True)
+            weight = jnp.where(member, jnp.exp(score - top), 0.0)
+            total = jnp.sum(weight, axis=1, keepdims=True)
+            acc_out[d, j * group_rows : (j + 1) * group_rows, :] = jnp.dot(
+                weight.astype(bf16), value, preferred_element_type=f32
+            ).astype(bf16)
+            stats.append(jnp.where(lane == 0, top, total))
+        stat_out[d] = jnp.concatenate(stats, axis=0).T[:8]
+        if d < n_tp - 1:
+            for copy in (
+                remote(stat_out.at[d], stat_in.at[d], stat_send.at[d], stat_recv.at[d], "tp", peer),
+                remote(acc_out.at[d], acc_in.at[d], acc_send.at[d], acc_recv.at[d], "tp", peer),
+            ):
+                copy.start()
+                acc_copies.append(copy)
+    for copy in acc_copies:
+        copy.wait()
+
+    stat_rows = jnp.concatenate(
+        [stat_in[d] for d in range(n_tp - 1)] + [stat_out[n_tp - 1]]
+        + [jnp.zeros((HS - 8 * n_tp, own_rows), f32)],
+        axis=0,
+    )
+    stat_columns = stat_rows.T
+    tops = [stat_columns[:, 8 * d : 8 * d + 1] for d in range(n_tp)]
+    totals = [stat_columns[:, 8 * d + 1 : 8 * d + 2] for d in range(n_tp)]
+    best = functools.reduce(jnp.maximum, tops, new_score)
+    fresh_ratio = jnp.exp(new_score - best)
+    numerator = fresh_ratio * fresh_value
+    denominator = fresh_ratio
+    for d in range(n_tp):
+        ratio = jnp.exp(tops[d] - best)
+        part = acc_in[d] if d < n_tp - 1 else acc_out[d]
+        numerator = numerator + ratio * part.astype(f32)
+        denominator = denominator + ratio * totals[d]
+    normal = numerator / denominator
+    attention = jnp.concatenate(
+        [normal[h * rows : (h + 1) * rows] for h in range(heads_here)], axis=1
+    ).astype(bf16)
+
+    weight_copies[0].wait()
+    per_lane = HS // rank
+    chunk = 2 * HS
+    chunk_lane = lax.broadcasted_iota(jnp.int32, (rows, HS), 1)
+    adapter = adapter_ref[...]
+    folded = jnp.zeros((rows, HS), f32)
+    for i in range(shrink_w.shape[0] // chunk):
+        part = lax.dot_general(
+            attention,
+            shrink_w[i * chunk : (i + 1) * chunk, :],
+            (((1,), (1,)), ((), ())),
+            preferred_element_type=f32,
+        )
+        for j in range(chunk // HS):
+            first = (i * chunk // HS + j) * per_lane
+            folded = folded + jnp.where(
+                adapter == first + chunk_lane // rank, part[:, j * HS : (j + 1) * HS], 0.0
+            )
+    shrink_out[...] = folded
+    shrink_copies = [
+        remote(
+            shrink_out, shrink_in.at[d], shrink_send.at[d], shrink_recv.at[d], "tp", peer
+        )
+        for d, peer in enumerate(tp_peers)
+    ]
+    for copy in shrink_copies:
+        copy.start()
+
+    step = 256
+    base_copies = []
+    for d, peer in enumerate(order):
+        weight_copies[1 + d].wait()
+
+        def tile(i, carry, d=d, peer=peer):
+            left = pl.multiple_of(peer * here + i * step, step)
+            right = pl.multiple_of(peer * here + half + i * step, step)
+            both = jnp.concatenate(
+                [
+                    jnp.dot(attention, out_w[:, pl.ds(at, step)], preferred_element_type=f32)
+                    for at in (left, right)
+                ],
+                axis=0,
+            )
+            if d < n_tp - 1:
+                base_out[d, :, pl.ds(pl.multiple_of(i * step, step), step)] = both.astype(bf16)
+            else:
+                result_ref[:, pl.ds(pl.multiple_of(i * step, step), step)] = both[:rows]
+                result_ref[:, pl.ds(pl.multiple_of(half + i * step, step), step)] = both[rows:]
+            return carry
+
+        lax.fori_loop(0, half // step, tile, 0)
+        if d < n_tp - 1:
+            copy = remote(
+                base_out.at[d], base_in.at[d], base_send.at[d], base_recv.at[d], "tp", peer
+            )
+            copy.start()
+            base_copies.append(copy)
+
+    for copy in shrink_copies:
+        copy.wait()
+    shrink = shrink_out[...]
+    for d in range(n_tp - 1):
+        shrink = shrink + shrink_in[d]
+    spread = jnp.concatenate(
+        [
+            jnp.where(adapter == c * per_lane + chunk_lane // rank, shrink, 0.0)
+            for c in range(shrink_w.shape[0] // HS)
+        ],
+        axis=1,
+    ).astype(bf16)
+    weight_copies[1 + n_tp].wait()
+
+    def expand_tile(i, carry):
+        at = pl.ds(pl.multiple_of(i * step, step), step)
+        result_ref[:, at] = result_ref[:, at] + adapter_factor * jnp.dot(
+            spread, expand_w[:, at], preferred_element_type=f32
+        )
+        return carry
+
+    lax.fori_loop(0, here // step, expand_tile, 0)
+    for copy in base_copies:
+        copy.wait()
+    for d in range(n_tp - 1):
+        arrived = base_in[d].astype(f32)
+        result_ref[:, :half] += arrived[:rows]
+        result_ref[:, half:] += arrived[rows:]
+
+
+def fused_body(
+    queries,
+    new_kv,
+    kv_cache,
+    slot_owner,
+    slot_fill,
+    mig_source,
+    mig_slot,
+    adapter_id,
+    out_weight,
+    shrink_weight,
+    expand_weight,
+):
+    f32, bf16, i32 = jnp.float32, jnp.bfloat16, jnp.int32
+    n_tp, n_rep = lax.axis_size("tp"), lax.axis_size("rep")
+    rows, here = queries.shape
+    heads_here = here // HS
+    slots = kv_cache.shape[1]
+    migs = mig_source.shape[1]
+    width = kv_cache.shape[3]
+    adapters, _, rank = shrink_weight.shape
+    query_rows = queries.reshape(rows, heads_here, HS).transpose(1, 0, 2).reshape(-1, HS)
+    own_rows = query_rows.shape[0]
+    used = jnp.arange(BLK, dtype=i32)[None, :] < slot_fill[0][:, None]
+    column_row = jnp.where(used, slot_owner[0][:, None], -1).reshape(1, slots * BLK)
+    slot_tile = jnp.broadcast_to(jnp.pad(mig_slot, ((0, 0), (0, HS - migs)))[:, None], (1, 8, HS))
+    vmem = pl.BlockSpec(memory_space=pltpu.VMEM)
+    smem = pl.BlockSpec(memory_space=pltpu.SMEM)
+    hbm = pl.BlockSpec(memory_space=pl.ANY)
+    dma = pltpu.SemaphoreType.DMA
+    peers, others = n_tp - 1, n_rep - 1
+    total = pl.pallas_call(
+        functools.partial(layer_kernel, n_tp, n_rep, rank),
+        out_shape=jax.ShapeDtypeStruct((rows, here), f32),
+        in_specs=[vmem, vmem, hbm, vmem, smem, vmem, vmem, hbm, hbm, hbm],
+        out_specs=vmem,
+        scratch_shapes=[
+            pltpu.VMEM((slots, BLK, width), bf16),
+            pltpu.VMEM(out_weight.shape, bf16),
+            pltpu.VMEM((adapters * rank, here), bf16),
+            pltpu.VMEM((adapters * rank, here), bf16),
+            pltpu.VMEM((n_tp * own_rows, HS), bf16),
+            pltpu.VMEM((n_rep, 8, HS), i32),
+            pltpu.SMEM((n_rep, 8, HS), i32),
+            pltpu.VMEM((others, migs, BLK, width), bf16),
+            pltpu.VMEM((n_rep, migs, BLK, width), bf16),
+            pltpu.VMEM((n_tp, own_rows, HS), bf16),
+            pltpu.VMEM((peers, own_rows, HS), bf16),
+            pltpu.VMEM((n_tp, 8, own_rows), f32),
+            pltpu.VMEM((peers, 8, own_rows), f32),
+            pltpu.VMEM((rows, HS), f32),
+            pltpu.VMEM((peers, rows, HS), f32),
+            pltpu.VMEM((peers, 2 * rows, here // 2), bf16),
+            pltpu.VMEM((peers, 2 * rows, here // 2), bf16),
+            dma,
+            dma((2 + n_tp,)),
+            dma,
+            dma((peers,)),
+            dma((peers,)),
+            dma((others,)),
+            dma((others,)),
+            dma((others,)),
+            dma((others,)),
+            dma((peers,)),
+            dma((peers,)),
+            dma((peers,)),
+            dma((peers,)),
+            dma((peers,)),
+            dma((peers,)),
+            dma((peers,)),
+            dma((peers,)),
+        ],
+        compiler_params=pltpu.CompilerParams(
+            collective_id=0, has_side_effects=True, vmem_limit_bytes=60 * 1024 * 1024
+        ),
+    )(
+        query_rows,
+        new_kv,
+        kv_cache[0],
+        column_row,
+        mig_source,
+        slot_tile,
+        adapter_id[:, None],
+        out_weight,
+        shrink_weight.transpose(0, 2, 1).reshape(adapters * rank, here),
+        expand_weight.reshape(adapters * rank, here),
+    )
+    return total.astype(bf16)
+
+
 def solution(mesh):
+    heads_here = H // mesh.shape["tp"]
+    fits = heads_here % (H // KVH) == 0
     return jax.shard_map(
-        body,
+        fused_body if fits else body,
         mesh=mesh,
         in_specs=(
             P(("parts", "rep"), "tp"),

time: 189 us -> 51.1 us (0.27)
  blocking collectives: 84.7 us -> 0 us
  Pallas kernels: 0 us -> 44.7 us
  matrix products: 41.4 us -> 0 us
  waiting for transfers between devices: 24.4 us -> 0 us
  between operations: 13.8 us -> 0.01 us
  local copies, waits for them, and re-layouts: 12.6 us -> 3.9 us
  other arithmetic: 8.18 us -> 2.32 us
  starting transfers between devices: 3.55 us -> 0 us
    all_gather x6 -> x0, blocking collectives: 67.9 us -> none  [the longest x2 27.7 us: joined(): everything = jax.tree.map(lambda part: lax.all_gather(part, axis), shard)]
    pallas_call x0 -> x1, Pallas kernels: none -> 44.7 us  [fused_body(): pl.pallas_call(functools.partial(layer_kernel, n_tp, n_rep, rank), out_sh...]
    dot_general x6 -> x0, matrix products: 41.2 us -> none  [the longest x1 13.7 us: body(): lax.dot_general(out_weight, attention, (((0,), (1,)), ((), ())), preferre...]
    all_gather x1 -> x0, waiting for transfers between devices: 24.3 us -> none  [joined(): everything = jax.tree.map(lambda part: lax.all_gather(part, axis), shard)]
    psum x1 -> x0, blocking collectives: 16.8 us -> none  [body(): shrink = lax.psum(partial_value, 'tp').astype(jnp.bfloat16)]
    add x7 -> x0, other arithmetic: 5.68 us -> none  [the longest x3 5.59 us: combine(): earlier[2] * first_ratio[..., None] + later[2] * second_ratio[..., None]]
    all_to_all x1 -> x0, starting transfers between devices: 3.47 us -> none  [body(): lax.all_to_all(packed, 'rep', split_axis=0, concat_axis=0, tiled=True)]
    slice x1 -> x0, local copies, waits for them, and re-layouts: 3.29 us -> none  [local_partials(): value_part = blocks[:, :, :, 1]]
  transfers between devices with their start and end apart: 3 -> 0, of which waited for: 1 -> 0; matrix products, arithmetic and copies ran while one was open for 8% -> 0% of each run, Pallas kernels for 0% -> 0%
where the time goes in v1:
time: 51.1 us; the launch traced here: 50.9 us
  Pallas kernels  44.7 us (87%)
  local copies, waits for them, and re-layouts  3.9 us (8%)
  other arithmetic  2.32 us (5%)
    pallas_call x1, Pallas kernels, fused_body(): pl.pallas_call(functools.partial(layer_kernel, n_tp, n_rep, rank), out_sh...  44.7 us
    convert_element_type x1, other arithmetic, fused_body(): return total.astype(bf16)  1.58 us
    broadcast_in_dim x1, local copies, waits for them, and re-layouts, fused_body(): adapter_id[:, None]  1.33 us
    broadcast_in_dim x2, local copies, waits for them, and re-layouts, fused_body(): jnp.broadcast_to(jnp.pad(mig_slot, ((0, 0), (0, HS - migs)))[:, None], (1...  1.28 us

profile of v1, /device:TPU:0, one launch (start us, length us, event | category | flops | bytes accessed | tf_op | source)
XLA Modules:
  0.0 50.9 jit_solution(16815028151418353994)
XLA Ops:
  0.0 0.0 copy-start
  0.0 0.7 %pad_bitcast_fusion = s32[128]{0:T(128)S(1)} fusion(s32[1,2]{1,0:T(1,128)} %param.17), kind=kLoop, calls=%fused_computation.3 | loop fusion | bytes 520 | tf_op jit(solution)/shard_map/broadcast_in_dim | solution.py:520
  0.7 0.6 %broadcast_in_dim.30.mig_slot_ref = s32[1,8,128]{2,1,0:T(8,128)} broadcast(s32[128]{0:T(128)S(1)} %pad_bitcast_fusion), dimensions={2} | broadcast | bytes 4608 | tf_op jit(solution)/shard_map/broadcast_in_dim | solution.py:520
  1.3 0.7 %fusion = s32[24,16]{1,0:T(8,128)S(1)} fusion(s32[24]{0:T(128)} %bitcast.23, s32[24]{0:T(128)} %bitcast.24), kind=kLoop, calls=%fused_computation.2 | loop fusion | flops 768 | bytes 1728 | tf_op jit(solution)/shard_map/jit(_where)/select_n | solution.py:519
  2.0 0.6 %select_n.15.column_row_ref = s32[1,384]{1,0:T(1,128)} reshape(s32[24,16]{1,0:T(8,128)S(1)} %fusion) | data formatting | bytes 3072 | tf_op jit(solution)/shard_map/jit(_where)/select_n | solution.py:519
  2.7 1.3 %copy.15.adapter_ref = s32[24,1]{1,0:T(8,128)} copy(s32[24,1]{0,1:T(1,128)} %bitcast.22) | data formatting | bytes 192 | tf_op jit(solution)/shard_map/broadcast_in_dim | solution.py:577
  4.0 0.0 copy-done
  4.0 0.7 %copy_bitcast_fusion = bf16[24,16,128]{2,0,1:T(8,128)(2,1)} fusion(bf16[24,2048]{1,0:T(8,128)(2,1)S(1)} %copy-done), kind=kLoop, calls=%fused_computation | loop fusion | bytes 196608 | tf_op jit(solution)/shard_map/reshape | solution.py:516
  4.6 44.7 %shard_map.109 = f32[24,2048]{1,0:T(8,128)} custom-call(bf16[384,128]{1,0:T(8,128)(2,1)} %bitcast.21, bf16[24,512]{1,0:T(8,128)(2,1)} %new_ref.1, bf16[24,16,2048]{2,1,0:T(8,128)(2,1)} %bitcast.20, s32[1,384]{1,0:T(1,128)} %select_n.15.column_row_ref, s32[1,2]{1,0:T(1,128)} %mig_source_ref.1, s32[1,8,128]{2,1,0:T(8,128)} %broadcast_in_dim.30.mig_slot_ref, ...), custom_call_target="tpu_custom_call" | custom-call | tf_op jit(solution)/shard_map/pallas_call | solution.py:526
  49.3 1.6 %convert_element_type.3 = bf16[24,2048]{1,0:T(8,128)(2,1)} convert(f32[24,2048]{1,0:T(8,128)} %shard_map.109) | non-fusion elementwise | flops 49152 | bytes 294912 | tf_op jit(solution)/shard_map/convert_element_type | solution.py:582
Async XLA Ops:
  0.0 4.0 %copy-start = (bf16[24,2048]{1,0:T(8,128)(2,1)S(1)}, bf16[24,2048]{1,0:T(8,128)(2,1)}, u32[]{:S(2)}) copy-start(bf16[24,2048]{1,0:T(8,128)(2,1)} %param.11) | copy-start | bytes 294916

commit v2 on v1

--- a/solution.py
+++ b/solution.py
@@ -185,6 +185,23 @@
     )
 
 
+def flipped(index, distance):
+    bit, other = 1, index
+    while bit <= distance:
+        if distance & bit:
+            other = other + bit - 2 * bit * lax.rem(index // bit, 2)
+        bit *= 2
+    return other
+
+
+def as_column(row):
+    size = row.shape[1]
+    same = lax.broadcasted_iota(jnp.int32, (size, size), 0) == lax.broadcasted_iota(
+        jnp.int32, (size, size), 1
+    )
+    return jnp.sum(jnp.where(same, row.astype(jnp.float32), 0.0), axis=1, keepdims=True)
+
+
 def layer_kernel(
     n_tp,
     n_rep,
@@ -192,7 +209,8 @@
     q_ref,
     new_ref,
     kv_hbm,
-    column_row_ref,
+    owner_ref,
+    fill_ref,
     mig_source_ref,
     mig_slot_ref,
     adapter_ref,
@@ -205,6 +223,7 @@
     shrink_w,
     expand_w,
     q_all,
+    slot_out,
     slot_in,
     slot_smem,
     mig_out,
@@ -217,6 +236,7 @@
     shrink_in,
     base_out,
     base_in,
+    sums,
     kv_sem,
     weight_sem,
     smem_sem,
@@ -243,15 +263,16 @@
     half = here // 2
     slots = kv.shape[0]
     migs = mig_out.shape[1]
-    own_rows = q_ref.shape[0]
-    heads_here = own_rows // rows
+    heads_here = here // HS
+    own_rows = heads_here * rows
     group_size = H // KVH
     groups_here = heads_here // group_size
     group_rows = rows * group_size
     score_scale = 1.0 / math.sqrt(HS)
-    tp_peers = [lax.rem(tp + d, n_tp) for d in range(1, n_tp)]
+    middle = n_tp // 2
+    tp_peers = [flipped(tp, d) for d in list(range(middle, n_tp)) + list(range(1, middle))]
     rep_peers = [lax.rem(rep + d, n_rep) for d in range(1, n_rep)]
-    kv_copy = pltpu.make_async_copy(kv_hbm, kv, kv_sem)
+    kv_copy = pltpu.make_async_copy(kv_hbm.at[0], kv, kv_sem)
     kv_copy.start()
     barrier = pltpu.get_barrier_semaphore()
     for peer in tp_peers:
@@ -281,24 +302,33 @@
     for copy in weight_copies:
         copy.start()
 
-    q_all[q_rows(tp), :] = q_ref[...]
-    slot_in[pl.ds(rep, 1)] = mig_slot_ref[...]
+    slot_lane = lax.broadcasted_iota(jnp.int32, slot_out.shape, 2)
+    wanted = jnp.zeros(slot_out.shape, jnp.int32)
+    for k in range(migs):
+        wanted = jnp.where(slot_lane == k, mig_slot_ref[0, k], wanted)
+    slot_out[...] = wanted
+    slot_in[pl.ds(rep, 1)] = wanted
+    own_query = q_ref[...].astype(f32)
+    own_query = jnp.concatenate(
+        [own_query[:, h * HS : (h + 1) * HS] for h in range(heads_here)], axis=0
+    )
+    q_all[q_rows(tp), :] = own_query.astype(bf16)
     mig_in[pl.ds(rep, 1)] = jnp.zeros((1,) + mig_in.shape[1:], bf16)
     pl.semaphore_wait(barrier, n_tp - 1 + n_rep - 1)
 
     slot_copies = [
         remote(
-            mig_slot_ref, slot_in.at[pl.ds(rep, 1)], slot_send.at[d], slot_recv.at[d], "rep", peer
+            slot_out, slot_in.at[pl.ds(rep, 1)], slot_send.at[d], slot_recv.at[d], "rep", peer
         )
         for d, peer in enumerate(rep_peers)
     ]
     for copy in slot_copies:
         copy.start()
     q_copies = [
-        remote(q_ref, q_all.at[q_rows(tp), :], q_send.at[d], q_recv.at[d], "tp", peer)
+        remote(q_all.at[q_rows(tp), :], q_all.at[q_rows(tp), :], q_send.at[d], q_recv.at[d], "tp", peer)
         for d, peer in enumerate(tp_peers)
     ]
-    for copy in q_copies[::-1]:
+    for copy in q_copies:
         copy.start()
 
     kv_copy.wait()
@@ -317,7 +347,6 @@
         copy.start()
         mig_copies.append(copy)
 
-    own_query = q_ref[...].astype(f32)
     fresh = new_ref[...].astype(f32)
     fresh_key = jnp.concatenate(
         [
@@ -337,10 +366,16 @@
     )
     new_score = jnp.sum(own_query * fresh_key, axis=1, keepdims=True) * score_scale
     row_index = lax.rem(lax.broadcasted_iota(jnp.int32, (group_rows, slots * BLK), 0), rows)
-    member = row_index == column_row_ref[...]
-
-    for copy in q_copies:
-        copy.wait()
+    slot_of = lax.broadcasted_iota(jnp.int32, (slots, slots * BLK), 1) // BLK
+    spot = lax.rem(lax.broadcasted_iota(jnp.int32, (1, slots * BLK), 1), BLK).astype(f32)
+    inside = slot_of == lax.broadcasted_iota(jnp.int32, (slots, slots * BLK), 0)
+    owner, fill = [
+        jnp.sum(jnp.where(inside, as_column(ref[...]), 0.0), axis=0, keepdims=True)
+        for ref in (owner_ref, fill_ref)
+    ]
+    member = row_index.astype(f32) == jnp.where(spot < fill, owner, -1.0)
+    adapter = as_column(adapter_ref[...])
+
     for copy in mig_copies:
         copy.wait()
     for k in range(migs):
@@ -349,6 +384,8 @@
     acc_copies = []
     lane = lax.broadcasted_iota(jnp.int32, (group_rows, HS), 1)
     for d, peer in enumerate(order):
+        if d < n_tp - 1:
+            q_copies[d].wait_recv()
         stats = []
         for j in range(groups_here):
             group = peer * groups_here + j
@@ -371,14 +408,27 @@
                 weight.astype(bf16), value, preferred_element_type=f32
             ).astype(bf16)
             stats.append(jnp.where(lane == 0, top, total))
+            if d < n_tp - 1:
+                part = pl.ds(j * group_rows, group_rows)
+                copy = remote(
+                    acc_out.at[d, part],
+                    acc_in.at[d, part],
+                    acc_send.at[d, j],
+                    acc_recv.at[d, j],
+                    "tp",
+                    peer,
+                )
+                copy.start()
+                acc_copies.append(copy)
         stat_out[d] = jnp.concatenate(stats, axis=0).T[:8]
         if d < n_tp - 1:
-            for copy in (
-                remote(stat_out.at[d], stat_in.at[d], stat_send.at[d], stat_recv.at[d], "tp", peer),
-                remote(acc_out.at[d], acc_in.at[d], acc_send.at[d], acc_recv.at[d], "tp", peer),
-            ):
-                copy.start()
-                acc_copies.append(copy)
+            copy = remote(
+                stat_out.at[d], stat_in.at[d], stat_send.at[d], stat_recv.at[d], "tp", peer
+            )
+            copy.start()
+            acc_copies.append(copy)
+    for copy in q_copies:
+        copy.wait_send()
     for copy in acc_copies:
         copy.wait()
 
@@ -404,37 +454,40 @@
         [normal[h * rows : (h + 1) * rows] for h in range(heads_here)], axis=1
     ).astype(bf16)
 
-    weight_copies[0].wait()
-    per_lane = HS // rank
-    chunk = 2 * HS
-    chunk_lane = lax.broadcasted_iota(jnp.int32, (rows, HS), 1)
-    adapter = adapter_ref[...]
-    folded = jnp.zeros((rows, HS), f32)
-    for i in range(shrink_w.shape[0] // chunk):
-        part = lax.dot_general(
-            attention,
-            shrink_w[i * chunk : (i + 1) * chunk, :],
-            (((1,), (1,)), ((), ())),
-            preferred_element_type=f32,
-        )
-        for j in range(chunk // HS):
-            first = (i * chunk // HS + j) * per_lane
-            folded = folded + jnp.where(
-                adapter == first + chunk_lane // rank, part[:, j * HS : (j + 1) * HS], 0.0
+    def send_shrink():
+        weight_copies[0].wait()
+        chunk = 2 * HS
+        folded = jnp.zeros((rank, rows), f32)
+        for i in range(shrink_w.shape[0] // chunk):
+            part = lax.dot_general(
+                shrink_w[i * chunk : (i + 1) * chunk, :],
+                attention,
+                (((1,), (1,)), ((), ())),
+                preferred_element_type=f32,
             )
-    shrink_out[...] = folded
-    shrink_copies = [
-        remote(
-            shrink_out, shrink_in.at[d], shrink_send.at[d], shrink_recv.at[d], "tp", peer
-        )
-        for d, peer in enumerate(tp_peers)
-    ]
-    for copy in shrink_copies:
-        copy.start()
+            for j in range(chunk // rank):
+                folded = folded + jnp.where(
+                    adapter_ref[...] == i * (chunk // rank) + j,
+                    part[j * rank : (j + 1) * rank],
+                    0.0,
+                )
+        shrink_out[...] = folded
+        copies = [
+            remote(
+                shrink_out, shrink_in.at[d], shrink_send.at[d], shrink_recv.at[d], "tp", peer
+            )
+            for d, peer in enumerate(tp_peers)
+        ]
+        for copy in copies:
+            copy.start()
+        return copies
 
     step = 256
     base_copies = []
+    shrink_copies = []
     for d, peer in enumerate(order):
+        if d == max(n_tp - 2, 0):
+            shrink_copies = send_shrink()
         weight_copies[1 + d].wait()
 
         def tile(i, carry, d=d, peer=peer):
@@ -450,8 +503,8 @@
             if d < n_tp - 1:
                 base_out[d, :, pl.ds(pl.multiple_of(i * step, step), step)] = both.astype(bf16)
             else:
-                result_ref[:, pl.ds(pl.multiple_of(i * step, step), step)] = both[:rows]
-                result_ref[:, pl.ds(pl.multiple_of(half + i * step, step), step)] = both[rows:]
+                sums[:, pl.ds(pl.multiple_of(i * step, step), step)] = both[:rows]
+                sums[:, pl.ds(pl.multiple_of(half + i * step, step), step)] = both[rows:]
             return carry
 
         lax.fori_loop(0, half // step, tile, 0)
@@ -467,9 +520,12 @@
     shrink = shrink_out[...]
     for d in range(n_tp - 1):
         shrink = shrink + shrink_in[d]
+    per_lane = HS // rank
+    shrink = jnp.concatenate([shrink] * per_lane, axis=0).T
+    chunk_lane = lax.broadcasted_iota(jnp.int32, (rows, HS), 1)
     spread = jnp.concatenate(
         [
-            jnp.where(adapter == c * per_lane + chunk_lane // rank, shrink, 0.0)
+            jnp.where(adapter == (c * per_lane + chunk_lane // rank).astype(f32), shrink, 0.0)
             for c in range(shrink_w.shape[0] // HS)
         ],
         axis=1,
@@ -478,7 +534,7 @@
 
     def expand_tile(i, carry):
         at = pl.ds(pl.multiple_of(i * step, step), step)
-        result_ref[:, at] = result_ref[:, at] + adapter_factor * jnp.dot(
+        sums[:, at] = sums[:, at] + adapter_factor * jnp.dot(
             spread, expand_w[:, at], preferred_element_type=f32
         )
         return carry
@@ -486,10 +542,13 @@
     lax.fori_loop(0, here // step, expand_tile, 0)
     for copy in base_copies:
         copy.wait()
+    left, right = sums[:, :half], sums[:, half:]
     for d in range(n_tp - 1):
         arrived = base_in[d].astype(f32)
-        result_ref[:, :half] += arrived[:rows]
-        result_ref[:, half:] += arrived[rows:]
+        left = left + arrived[:rows]
+        right = right + arrived[rows:]
+    result_ref[:, :half] = left.astype(bf16)
+    result_ref[:, half:] = right.astype(bf16)
 
 
 def fused_body(
@@ -513,20 +572,16 @@
     migs = mig_source.shape[1]
     width = kv_cache.shape[3]
     adapters, _, rank = shrink_weight.shape
-    query_rows = queries.reshape(rows, heads_here, HS).transpose(1, 0, 2).reshape(-1, HS)
-    own_rows = query_rows.shape[0]
-    used = jnp.arange(BLK, dtype=i32)[None, :] < slot_fill[0][:, None]
-    column_row = jnp.where(used, slot_owner[0][:, None], -1).reshape(1, slots * BLK)
-    slot_tile = jnp.broadcast_to(jnp.pad(mig_slot, ((0, 0), (0, HS - migs)))[:, None], (1, 8, HS))
+    own_rows = rows * heads_here
     vmem = pl.BlockSpec(memory_space=pltpu.VMEM)
     smem = pl.BlockSpec(memory_space=pltpu.SMEM)
     hbm = pl.BlockSpec(memory_space=pl.ANY)
     dma = pltpu.SemaphoreType.DMA
     peers, others = n_tp - 1, n_rep - 1
-    total = pl.pallas_call(
+    return pl.pallas_call(
         functools.partial(layer_kernel, n_tp, n_rep, rank),
-        out_shape=jax.ShapeDtypeStruct((rows, here), f32),
-        in_specs=[vmem, vmem, hbm, vmem, smem, vmem, vmem, hbm, hbm, hbm],
+        out_shape=jax.ShapeDtypeStruct((rows, here), bf16),
+        in_specs=[vmem, vmem, hbm, vmem, vmem, smem, smem, vmem, hbm, hbm, hbm],
         out_specs=vmem,
         scratch_shapes=[
             pltpu.VMEM((slots, BLK, width), bf16),
@@ -534,6 +589,7 @@
             pltpu.VMEM((adapters * rank, here), bf16),
             pltpu.VMEM((adapters * rank, here), bf16),
             pltpu.VMEM((n_tp * own_rows, HS), bf16),
+            pltpu.VMEM((1, 8, HS), i32),
             pltpu.VMEM((n_rep, 8, HS), i32),
             pltpu.SMEM((n_rep, 8, HS), i32),
             pltpu.VMEM((others, migs, BLK, width), bf16),
@@ -542,10 +598,11 @@
             pltpu.VMEM((peers, own_rows, HS), bf16),
             pltpu.VMEM((n_tp, 8, own_rows), f32),
             pltpu.VMEM((peers, 8, own_rows), f32),
-            pltpu.VMEM((rows, HS), f32),
-            pltpu.VMEM((peers, rows, HS), f32),
+            pltpu.VMEM((rank, rows), f32),
+            pltpu.VMEM((peers, rank, rows), f32),
             pltpu.VMEM((peers, 2 * rows, here // 2), bf16),
             pltpu.VMEM((peers, 2 * rows, here // 2), bf16),
+            pltpu.VMEM((rows, here), f32),
             dma,
             dma((2 + n_tp,)),
             dma,
@@ -555,8 +612,8 @@
             dma((others,)),
             dma((others,)),
             dma((others,)),
-            dma((peers,)),
-            dma((peers,)),
+            dma((peers, heads_here * KVH // H)),
+            dma((peers, heads_here * KVH // H)),
             dma((peers,)),
             dma((peers,)),
             dma((peers,)),
@@ -568,18 +625,18 @@
             collective_id=0, has_side_effects=True, vmem_limit_bytes=60 * 1024 * 1024
         ),
     )(
-        query_rows,
+        queries,
         new_kv,
-        kv_cache[0],
-        column_row,
+        kv_cache,
+        slot_owner,
+        slot_fill,
         mig_source,
-        slot_tile,
-        adapter_id[:, None],
+        mig_slot,
+        adapter_id[None, :],
         out_weight,
         shrink_weight.transpose(0, 2, 1).reshape(adapters * rank, here),
         expand_weight.reshape(adapters * rank, here),
     )
-    return total.astype(bf16)
 
 
 def solution(mesh):

time: 51.1 us -> 47 us (0.920)
  local copies, waits for them, and re-layouts: 3.9 us -> 1.54 us
  other arithmetic: 2.32 us -> 0 us
  Pallas kernels: 44.7 us -> 45.3 us
    broadcast_in_dim x3 -> x0, local copies, waits for them, and re-layouts: 2.61 us -> none  [the longest x1 1.33 us: fused_body(): adapter_id[:, None]]
    convert_element_type x1 -> x0, other arithmetic: 1.58 us -> none  [fused_body(): return total.astype(bf16)]
    unnamed x2 -> x1, local copies, waits for them, and re-layouts: 0.01 us -> 1.54 us
    select_n x1 -> x0, other arithmetic: 0.74 us -> none  [fused_body(): jnp.where(used, slot_owner[0][:, None], -1).reshape(1, slots * BLK)]
    reshape x1 -> x0, local copies, waits for them, and re-layouts: 0.66 us -> none  [fused_body(): queries.reshape(rows, heads_here, HS).transpose(1, 0, 2).reshape(-1, HS)]
    select_n x1 -> x0, local copies, waits for them, and re-layouts: 0.63 us -> none  [fused_body(): jnp.where(used, slot_owner[0][:, None], -1).reshape(1, slots * BLK)]
    pallas_call x1, Pallas kernels: 44.7 us -> 45.3 us  [fused_body(): pl.pallas_call(functools.partial(layer_kernel, n_tp, n_rep, rank), out_sh...]
where the time goes in v2:
time: 47 us; the launch traced here: 46.8 us
  Pallas kernels  45.3 us (96%)
  local copies, waits for them, and re-layouts  1.54 us (3%)
    pallas_call x1, Pallas kernels, fused_body(): pl.pallas_call(functools.partial(layer_kernel, n_tp, n_rep, rank), out_sh...  45.3 us
    unnamed x1, local copies, waits for them, and re-layouts  1.54 us

profile of v2, /device:TPU:0, one launch (start us, length us, event | category | flops | bytes accessed | tf_op | source)
XLA Modules:
  0.0 46.8 jit_solution(9804731470965041011)
XLA Ops:
  0.0 45.3 %shard_map.109 = bf16[24,2048]{1,0:T(8,128)(2,1)} custom-call(bf16[24,2048]{1,0:T(8,128)(2,1)} %q_ref.1, bf16[24,512]{1,0:T(8,128)(2,1)} %new_ref.1, bf16[1,24,16,2048]{3,2,1,0:T(8,128)(2,1)} %kv_hbm.1, s32[1,24]{1,0:T(1,128)} %owner_ref.1, s32[1,24]{1,0:T(1,128)} %fill_ref.1, s32[1,2]{1,0:T(1,128)} %mig_source_ref.1, s32[1,2]{1,0:T(1,128)} %mig_slot_ref.1, ...), custom_call_target="tpu_custom_call" | custom-call | tf_op jit(solution)/shard_map/pallas_call | solution.py:581
  45.3 1.5 %copy.13 = bf16[24,2048]{1,0:T(8,128)(2,1)} copy(bf16[24,2048]{1,0:T(8,128)(2,1)} %shard_map.109) | data formatting | bytes 196608

commit v3 on v2

--- a/solution.py
+++ b/solution.py
@@ -486,7 +486,7 @@
     base_copies = []
     shrink_copies = []
     for d, peer in enumerate(order):
-        if d == max(n_tp - 2, 0):
+        if d == min(1, n_tp - 1):
             shrink_copies = send_shrink()
         weight_copies[1 + d].wait()
 

time: 47 us -> 45 us (0.957)
  Pallas kernels: 45.3 us -> 43.3 us
    pallas_call x1, Pallas kernels: 45.3 us -> 43.3 us  [fused_body(): pl.pallas_call(functools.partial(layer_kernel, n_tp, n_rep, rank), out_sh...]
where the time goes in v3:
time: 45 us; the launch traced here: 44.9 us
  Pallas kernels  43.3 us (96%)
  local copies, waits for them, and re-layouts  1.54 us (3%)
    pallas_call x1, Pallas kernels, fused_body(): pl.pallas_call(functools.partial(layer_kernel, n_tp, n_rep, rank), out_sh...  43.3 us
    unnamed x1, local copies, waits for them, and re-layouts  1.54 us

profile of v3, /device:TPU:0, one launch (start us, length us, event | category | flops | bytes accessed | tf_op | source)
XLA Modules:
  0.0 44.9 jit_solution(12419581894159080736)
XLA Ops:
  0.0 43.3 %shard_map.109 = bf16[24,2048]{1,0:T(8,128)(2,1)} custom-call(bf16[24,2048]{1,0:T(8,128)(2,1)} %q_ref.1, bf16[24,512]{1,0:T(8,128)(2,1)} %new_ref.1, bf16[1,24,16,2048]{3,2,1,0:T(8,128)(2,1)} %kv_hbm.1, s32[1,24]{1,0:T(1,128)} %owner_ref.1, s32[1,24]{1,0:T(1,128)} %fill_ref.1, s32[1,2]{1,0:T(1,128)} %mig_source_ref.1, s32[1,2]{1,0:T(1,128)} %mig_slot_ref.1, ...), custom_call_target="tpu_custom_call" | custom-call | tf_op jit(solution)/shard_map/pallas_call | solution.py:581
  43.3 1.5 %copy.13 = bf16[24,2048]{1,0:T(8,128)(2,1)} copy(bf16[24,2048]{1,0:T(8,128)(2,1)} %shard_map.109) | data formatting | bytes 196608

commit v4 on v3

--- a/solution.py
+++ b/solution.py
@@ -271,7 +271,11 @@
     score_scale = 1.0 / math.sqrt(HS)
     middle = n_tp // 2
     tp_peers = [flipped(tp, d) for d in list(range(middle, n_tp)) + list(range(1, middle))]
-    rep_peers = [lax.rem(rep + d, n_rep) for d in range(1, n_rep)]
+    if n_rep & (n_rep - 1):
+        rep_peers = [lax.rem(rep + d, n_rep) for d in range(1, n_rep)]
+    else:
+        far = n_rep // 2
+        rep_peers = [flipped(rep, d) for d in list(range(far, n_rep)) + list(range(1, far))]
     kv_copy = pltpu.make_async_copy(kv_hbm.at[0], kv, kv_sem)
     kv_copy.start()
     barrier = pltpu.get_barrier_semaphore()
@@ -539,7 +543,7 @@
         )
         return carry
 
-    lax.fori_loop(0, here // step, expand_tile, 0)
+    lax.fori_loop(0, here // step, expand_tile, 0, unroll=True)
     for copy in base_copies:
         copy.wait()
     left, right = sums[:, :half], sums[:, half:]

time: 45 us -> 44.7 us (level)
  no operation moved by 1% of the time
where the time goes in v4:
time: 44.7 us; the launch traced here: 44.5 us
  Pallas kernels  43 us (96%)
  local copies, waits for them, and re-layouts  1.54 us (3%)
    pallas_call x1, Pallas kernels, fused_body(): pl.pallas_call(functools.partial(layer_kernel, n_tp, n_rep, rank), out_sh...  43 us
    unnamed x1, local copies, waits for them, and re-layouts  1.54 us

profile of v4, /device:TPU:0, one launch (start us, length us, event | category | flops | bytes accessed | tf_op | source)
XLA Modules:
  0.0 44.5 jit_solution(11420404005593766196)
XLA Ops:
  0.0 43.0 %shard_map.109 = bf16[24,2048]{1,0:T(8,128)(2,1)} custom-call(bf16[24,2048]{1,0:T(8,128)(2,1)} %q_ref.1, bf16[24,512]{1,0:T(8,128)(2,1)} %new_ref.1, bf16[1,24,16,2048]{3,2,1,0:T(8,128)(2,1)} %kv_hbm.1, s32[1,24]{1,0:T(1,128)} %owner_ref.1, s32[1,24]{1,0:T(1,128)} %fill_ref.1, s32[1,2]{1,0:T(1,128)} %mig_source_ref.1, s32[1,2]{1,0:T(1,128)} %mig_slot_ref.1, ...), custom_call_target="tpu_custom_call" | custom-call | tf_op jit(solution)/shard_map/pallas_call | solution.py:585
  43.0 1.5 %copy.13 = bf16[24,2048]{1,0:T(8,128)(2,1)} copy(bf16[24,2048]{1,0:T(8,128)(2,1)} %shard_map.109) | data formatting | bytes 196608
